TPU v7x, 256 devices: a whole 4x4x8 slice. The times are simulated.
256 devices in a mesh: pipe: 16 (over y_hi, z), dp: 16 (over x, y_lo, core).
Axes of the slice: x: 4, y: 4 (y_hi: 2, y_lo: 2; y = y_hi * 2 + y_lo), z: 8, core: 2. Of those that a mesh axis runs over, the one named last changes fastest.
Arguments:
- stash: bfloat16 [16, 2048, 12288], P('pipe', 'dp'), may hold values from -6 to 6
- grad_in: bfloat16 [16, 2048, 12288], P('pipe', 'dp'), may hold values from -6 to 6
- base_back: bfloat16 [16, 2048, 12288], P('pipe', 'dp'), may hold values from -6 to 6
- gain: bfloat16 [16, 12288], P('pipe'), may hold values from 0.5 to 1.5
- w_down: bfloat16 [16, 64, 12288], P('pipe', None, 'dp'), may hold values from -0.75 to 0.75
- w_up: bfloat16 [16, 64, 12288], P('pipe', None, 'dp'), may hold values from -0.0546875 to 0.0546875
- mom_down: bfloat16 [16, 64, 12288], P('pipe', None, 'dp'), may hold values from -0.046875 to 0.046875
- mom_up: bfloat16 [16, 64, 12288], P('pipe', None, 'dp'), may hold values from -0.4375 to 0.4375
Outputs:
- grad_prev: bfloat16 [16, 2048, 12288], P('pipe', 'dp')
- step_first: bfloat16 [16, 64, 12288], P('pipe', None, 'dp')
- step_second: bfloat16 [16, 64, 12288], P('pipe', None, 'dp')
- moment_first: bfloat16 [16, 64, 12288], P('pipe', None, 'dp')
- moment_second: bfloat16 [16, 64, 12288], P('pipe', None, 'dp')
All inputs are finite; a program needn't handle non-finite values.
Results may differ from a plain program's by a relative error of at most 0.039.
Values may be sent and summed in bfloat16 or wider, within the bound.
A program may use at most 64 MiB of HBM per device.

v0:
```python
import jax
import jax.numpy as jnp
from jax import lax
from jax.sharding import PartitionSpec as P

norm_eps = 1e-05
beta_one = 0.9
beta_two = 0.99
lion_delta = 0.003
contract_last = (((1,), (1,)), ((), ()))
contract_first = (((0,), (0,)), ((), ()))


def swapped(array, axis, bit):
    return lax.ppermute(array, axis, [(i, i ^ 1 << bit) for i in range(lax.axis_size(axis))])


def shifted(block, axis, distance):
    devices = range(lax.axis_size(axis))
    route = [(i - distance, i) for i in devices if i - distance in devices]
    return lax.ppermute(block, axis, route)


def normalize(saved_rows, gain_row):
    values = saved_rows.astype(jnp.float32)
    average = jnp.mean(values, axis=-1, keepdims=True)
    centred = values - average
    variance = jnp.mean(centred * centred, axis=-1, keepdims=True)
    inverse = lax.rsqrt(variance + norm_eps)
    unit_rows = centred * inverse
    normed = (unit_rows * gain_row).astype(jnp.bfloat16)
    return (unit_rows, inverse, normed)


def norm_backward(back_norm, gain_row, unit_rows, inverse):
    scaled = back_norm * gain_row
    first_mean = jnp.mean(scaled, axis=-1, keepdims=True)
    second_mean = jnp.mean(scaled * unit_rows, axis=-1, keepdims=True)
    return (inverse * (scaled - first_mean - unit_rows * second_mean)).astype(jnp.bfloat16)


def lion(moment, gradient):
    blend = beta_one * moment + (1.0 - beta_one) * gradient
    direction = (blend / (jnp.abs(blend) + lion_delta)).astype(jnp.bfloat16)
    renewed = (beta_two * moment + (1.0 - beta_two) * gradient).astype(jnp.bfloat16)
    return (direction, renewed)


def shards(stash, grad_in, base_back, gain, w_down, w_up, mom_down, mom_up):
    top_bit = lax.axis_size("pipe").bit_length() - 2
    saved_rows = swapped(stash[0], "pipe", top_bit)
    grad_rows = grad_in[0]
    gain_row = gain[0].astype(jnp.float32)
    row_count = saved_rows.shape[0]
    rank_count = w_down.shape[1]
    unit_rows, inverse, normed = normalize(saved_rows, gain_row)
    down_full, up_full = (
        lax.all_gather(w_down[0], "dp", axis=1, tiled=True),
        lax.all_gather(w_up[0], "dp", axis=1, tiled=True),
    )
    low_float = lax.dot_general(
        normed, down_full, contract_last, preferred_element_type=jnp.float32
    )
    low_rows = low_float.astype(jnp.bfloat16)
    back_low = lax.dot_general(
        grad_rows, up_full, contract_last, preferred_element_type=jnp.float32
    )
    delta_rows = back_low.astype(jnp.bfloat16)
    adapter_back = jnp.dot(delta_rows, down_full, preferred_element_type=jnp.float32)
    back_norm = base_back[0].astype(jnp.float32) + adapter_back
    grad_input = norm_backward(back_norm, gain_row, unit_rows, inverse)
    upstream = shifted(grad_input, "pipe", -1)
    tokens_all = row_count * lax.axis_size("dp")
    first_full = lax.dot_general(
        normed, delta_rows, contract_first, preferred_element_type=jnp.float32
    )
    second_full = lax.dot_general(
        grad_rows, low_rows, contract_first, preferred_element_type=jnp.float32
    )
    whole_terms = jnp.concatenate([first_full, second_full], axis=1) / tokens_all
    shares = lax.psum_scatter(
        whole_terms.astype(jnp.bfloat16), "dp", scatter_dimension=0, tiled=True
    ).astype(jnp.float32)
    grad_first = shares[:, :rank_count].T
    grad_second = shares[:, rank_count:].T
    step_first, moment_first = lion(mom_down[0].astype(jnp.float32), grad_first)
    step_second, moment_second = lion(mom_up[0].astype(jnp.float32), grad_second)
    return (
        upstream[None],
        step_first[None],
        step_second[None],
        moment_first[None],
        moment_second[None],
    )


def solution(mesh):
    in_specs = (
        P("pipe", "dp", None),
        P("pipe", "dp", None),
        P("pipe", "dp", None),
        P("pipe", None),
        P("pipe", None, "dp"),
        P("pipe", None, "dp"),
        P("pipe", None, "dp"),
        P("pipe", None, "dp"),
    )
    out_specs = (
        P("pipe", "dp", None),
        P("pipe", None, "dp"),
        P("pipe", None, "dp"),
        P("pipe", None, "dp"),
        P("pipe", None, "dp"),
    )
    return jax.shard_map(shards, mesh=mesh, in_specs=in_specs, out_specs=out_specs, check_vma=False)
```

profile of v0, /device:TPU:255, one launch (start us, length us, event | category | flops | bytes accessed | tf_op | source)
XLA Modules:
  0.0 264.5 jit_solution(12618921307219543139)
XLA Ops:
  7.2 0.0 copy-start
  7.2 0.0 all-gather.5.cloned.1.call-start
  7.2 0.7 all-gather.5.cloned.1.call-update
  7.9 0.0 all-gather.7.cloned.1.call-start
  8.0 1.0 collective-permute-start
  9.0 0.0 all-gather.7.cloned.1.call-update
  9.0 0.0 reduce-scatter.2.cloned.1.call-start
  9.1 0.9 mul.123
  9.9 36.4 %all-gather.5.cloned.1.call-done = bf16[1,64,12288]{2,1,0:T(8,128)(2,1)} async-done(((bf16[1,64,768]{2,1,0:T(8,128)(2,1)}), bf16[1,64,12288]{2,1,0:T(8,128)(2,1)}) %all-gather.5.cloned.1.call-update) | async-done | bytes 1572880 | tf_op jit(solution)/shard_map/all_gather | solution.py:59
  46.4 0.0 copy-done
  46.4 2.6 fusion.25
  49.0 44.6 %collective-permute-done = bf16[128,12288]{1,0:T(8,128)(2,1)} collective-permute-done((bf16[128,12288]{1,0:T(8,128)(2,1)}, bf16[128,12288]{1,0:T(8,128)(2,1)}, u32[]{:S(2)}, u32[]{:S(2)}) %collective-permute-start) | collective-permute-done | bytes 3145760 | tf_op jit(solution)/shard_map/ppermute | solution.py:15
  93.6 2.4 convert_reduce_fusion
  96.0 2.9 %fusion.11 = f32[128]{0:T(128)S(1)} fusion(bf16[128,12288]{1,0:T(8,128)(2,1)} %collective-permute-done, f32[128]{0:T(128)S(1)} %broadcast_multiply_fusion.2), kind=kLoop, calls=%fused_computation.15 | loop fusion | flops 6291328 | bytes 3146752 | tf_op jit(solution)/shard_map/reduce_sum | solution.py:28
  98.9 0.0 all-gather.7.cloned.1.call-done
  98.9 5.8 %fusion.44 = (f32[128]{0:T(128)S(1)}, f32[128]{0:T(128)S(1)}, f32[128,12288]{1,0:T(8,128)S(1)}) fusion(f32[128]{0:T(128)S(1)} %add_rsqrt_fusion, f32[128]{0:T(128)S(1)} %broadcast_multiply_fusion.2, bf16[128,12288]{1,0:T(8,128)(2,1)} %collective-permute-done, f32[12288]{0:T(1024)S(1)} %bitcast.95, bf16[128,64]{0,1:T(8,128)(2,1)S(1)} %fusion.25, ...), kind=kOutput, calls=%fused_computation.51 | convolution fusion | flops 215482112 | bytes 14223360 | tf_op jit(solution)/shard_map/dot_general | solution.py:69
  104.7 4.6 %fusion.10 = (bf16[128,12288]{1,0:T(8,128)(2,1)S(1)}, bf16[128,12288]{1,0:T(8,128)(2,1)}) fusion(bf16[128,12288]{1,0:T(8,128)(2,1)} %collective-permute-done, f32[12288]{0:T(1024)S(1)} %bitcast.96, f32[128]{0:T(128)S(1)} %add_rsqrt_fusion, f32[128]{0:T(128)S(1)} %broadcast_multiply_fusion.2, f32[128]{0:T(128)S(1)} %get-tuple-element.16, ...), kind=kLoop, calls=%fused_computation.14 | loop fusion | flops 15728640 | bytes 15779840 | tf_op jit(solution)/shard_map/convert_element_type | solution.py:31
  109.3 0.0 copy-start.1
  109.3 1.7 copy-done.1
  111.0 2.2 fusion.45
  113.2 6.3 %convolution_bitcast_fusion = f32[12288,64]{0,1:T(8,128)} fusion(bf16[1,128,12288]{2,1,0:T(8,128)(2,1)S(1)} %copy-done, bf16[128,12288]{1,0:T(8,128)(2,1)} %copy-done.1, bf16[1,64,12288]{2,1,0:T(8,128)(2,1)} %all-gather.7.cloned.1.call-done), kind=kOutput, calls=%fused_computation.2 | convolution fusion | flops 402661376 | bytes 11010048 | tf_op jit(solution)/shard_map/dot_general | solution.py:77
  119.6 4.9 %fusion.12 = bf16[12288,128]{0,1:T(8,128)(2,1)} fusion(f32[12288,64]{0,1:T(8,128)} %convolution_bitcast_fusion, f32[12288,64]{0,1:T(8,128)} %fusion.45), kind=kLoop, calls=%fused_computation.17 | loop fusion | flops 4718592 | bytes 9437184 | tf_op jit(solution)/shard_map/convert_element_type | solution.py:82
  124.5 0.0 copy-start.2
  124.5 0.0 reduce-scatter.2.cloned.1.call-update
  124.5 4.4 %collective-permute-start.1 = (bf16[128,12288]{1,0:T(8,128)(2,1)}, bf16[128,12288]{1,0:T(8,128)(2,1)}, u32[]{:S(2)}, u32[]{:S(2)}) collective-permute-start(bf16[128,12288]{1,0:T(8,128)(2,1)} %get-tuple-element.8), channel_id=1, source_target_pairs={{16,0},{32,16},{48,32},{64,48},{80,64},{96,80},{112,96},{128,112},... | collective-permute-start | bytes 9437192 | tf_op jit(solution)/shard_map/ppermute | solution.py:21
  128.9 64.5 %collective-permute-done.1 = bf16[128,12288]{1,0:T(8,128)(2,1)} collective-permute-done((bf16[128,12288]{1,0:T(8,128)(2,1)}, bf16[128,12288]{1,0:T(8,128)(2,1)}, u32[]{:S(2)}, u32[]{:S(2)}) %collective-permute-start.1) | collective-permute-done | bytes 3145760 | tf_op jit(solution)/shard_map/ppermute | solution.py:21
  193.4 58.9 %reduce-scatter.2.cloned.1.call-done = bf16[768,128]{0,1:T(8,128)(2,1)} async-done(((bf16[12288,128]{0,1:T(8,128)(2,1)}), bf16[768,128]{0,1:T(8,128)(2,1)}) %reduce-scatter.2.cloned.1.call-update) | async-done | bytes 196624 | tf_op jit(solution)/shard_map/reduce_scatter | solution.py:81
  252.3 1.0 convert_element_type.58
  253.3 0.0 copy-done.2
  253.3 0.0 copy-done.3
  253.3 0.9 fusion.40
  254.2 3.8 %copy.14 = bf16[1,128,12288]{2,1,0:T(8,128)(2,1)} copy(bf16[1,128,12288]{2,1,0:T(8,128)(2,1)} %bitcast.6) | data formatting | bytes 6291456
  (4 shorter events, 0.0 us)
Async XLA Ops:
  7.2 39.2 %copy-start = (bf16[1,128,12288]{2,1,0:T(8,128)(2,1)S(1)}, bf16[1,128,12288]{2,1,0:T(8,128)(2,1)}, u32[]{:S(2)}) copy-start(bf16[1,128,12288]{2,1,0:T(8,128)(2,1)} %param.9) | copy-start | bytes 9437188
  7.2 39.2 %all-gather.5.cloned.1.call-start = ((), (), s32[]{:S(2)}) async-start(), calls=%async_computation.2 | async-start | bytes 1671168 | tf_op jit(solution)/shard_map/all_gather | solution.py:59
  7.9 91.0 %all-gather.7.cloned.1.call-start = ((), (), s32[]{:S(2)}) async-start(), calls=%async_computation.3 | async-start | bytes 1671168 | tf_op jit(solution)/shard_map/all_gather | solution.py:58
  8.0 85.6 %collective-permute-start = (bf16[128,12288]{1,0:T(8,128)(2,1)}, bf16[128,12288]{1,0:T(8,128)(2,1)}, u32[]{:S(2)}, u32[]{:S(2)}) collective-permute-start(bf16[128,12288]{1,0:T(8,128)(2,1)} %bitcast.97), channel_id=1, source_target_pairs={{0,128},{16,144},{32,160},{48,176},{64,192},{80,208},{96,224},{112... | collective-permute-start | bytes 9437192 | tf_op jit(solution)/shard_map/ppermute | solution.py:15
  9.0 243.3 %reduce-scatter.2.cloned.1.call-start = ((), (), s32[]{:S(2)}) async-start(), calls=%async_computation.1 | async-start | bytes 3342336 | tf_op jit(solution)/shard_map/reduce_scatter | solution.py:81
  109.3 1.7 copy-start.1
  124.5 128.8 %copy-start.2 = (bf16[1,64,768]{2,1,0:T(8,128)(2,1)S(1)}, bf16[1,64,768]{2,1,0:T(8,128)(2,1)}, u32[]{:S(2)}) copy-start(bf16[1,64,768]{2,1,0:T(8,128)(2,1)} %param.15) | copy-start | bytes 294916
  124.5 128.8 %copy-start.3 = (bf16[1,64,768]{2,1,0:T(8,128)(2,1)S(1)}, bf16[1,64,768]{2,1,0:T(8,128)(2,1)}, u32[]{:S(2)}) copy-start(bf16[1,64,768]{2,1,0:T(8,128)(2,1)} %param.14) | copy-start | bytes 294916
  124.5 68.9 %collective-permute-start.1 = (bf16[128,12288]{1,0:T(8,128)(2,1)}, bf16[128,12288]{1,0:T(8,128)(2,1)}, u32[]{:S(2)}, u32[]{:S(2)}) collective-permute-start(bf16[128,12288]{1,0:T(8,128)(2,1)} %get-tuple-element.8), channel_id=1, source_target_pairs={{16,0},{32,16},{48,32},{64,48},{80,64},{96,80},{112,96},{128,112},... | collective-permute-start | bytes 9437192 | tf_op jit(solution)/shard_map/ppermute | solution.py:21
Sparse Core Ops, SparseCore 0:
  9.8 36.4 all-gather.4
  48.2 37.6 all-gather.6
  124.6 127.6 reduce-scatter.1
where the time goes:
time: 265 us
  waiting for transfers between devices  205 us (77%)
  other arithmetic  17.5 us (7%)
  matrix products  17 us (6%)
  between operations  13.8 us (5%)
  starting transfers between devices  5.56 us (2%)
  local copies, waits for them, and re-layouts  5.54 us (2%)
    ppermute x1, waiting for transfers between devices, shifted(): return lax.ppermute(block, axis, route)  64.5 us
    reduce_scatter x1, waiting for transfers between devices, shards(): lax.psum_scatter(whole_terms.astype(jnp.bfloat16), 'dp', scatter_dimensio...  58.9 us
    ppermute x1, waiting for transfers between devices, swapped(): lax.ppermute(array, axis, [(i, i ^ 1 << bit) for i in range(lax.axis_size...  44.6 us
    all_gather x1, waiting for transfers between devices, shards(): lax.all_gather(w_up[0], 'dp', axis=1, tiled=True)  36.4 us
    dot_general x1, matrix products, shards(): lax.dot_general(grad_rows, low_rows, contract_first, preferred_element_ty...  6.31 us
    dot_general x1, matrix products, shards(): jnp.dot(delta_rows, down_full, preferred_element_type=jnp.float32)  5.78 us
    unnamed x9, local copies, waits for them, and re-layouts  5.54 us
  transfers between devices with their start and end apart: 5, of which 4 were waited for; matrix products, arithmetic and copies ran while one was open for 3% of the time, Pallas kernels for 0%

commit v1 on v0

v1 whole, which is shorter than its diff:
```python
import functools

import jax
import jax.numpy as jnp
from jax import lax
from jax.experimental import pallas as pl
from jax.experimental.pallas import tpu as pltpu
from jax.sharding import PartitionSpec as P

norm_eps = 1e-05
beta_one = 0.9
beta_two = 0.99
lion_delta = 0.003

D = 12288
RANK = 64
ROWS = 128
TOKENS = 2048
SHARE = D // 16
CHUNK = 16
CHUNKS = ROWS // CHUNK
WIDE = 1536
WIDES = D // WIDE
MESH = pl.DeviceIdType.MESH
f32 = jnp.float32
bf16 = jnp.bfloat16

contract_last = (((1,), (1,)), ((), ()))


def dot_last(a, b):
    return lax.dot_general(a, b, contract_last, preferred_element_type=f32)


def fold(v):
    parts = [v[:, i : i + 128] for i in range(0, v.shape[1], 128)]
    while len(parts) > 1:
        half = [a + b for a, b in zip(parts[::2], parts[1::2])]
        if len(parts) % 2:
            half.append(parts[-1])
        parts = half
    return parts[0]


def row_sum(acc):
    return jnp.sum(acc, axis=1, keepdims=True)


def main_kernel(
    stash, grad, base, gain, w_down, w_up,
    gp, g1_out, g2_out,
    st, sv, gr, ba, b, W, WS, gain_own, gain_far,
    delta_own, delta_far, low_own, low_far, b_mean, inv_row,
    part_send, part_keep, part_recv, sum_send, sum_recv,
    cross_send, cross_recv, pair_send, pair_recv, kept,
    local_sem, send_sem, recv_sem,
):
    s = lax.axis_index("pipe")
    d = lax.axis_index("dp")
    x, yl, c = d // 4, (d // 2) % 2, d % 2
    far = (s + 8) % 16
    z = s % 8
    z_down = s - z + (z + 7) % 8
    z_up = s - z + (z + 1) % 8
    d_pair = d + 2 - 4 * yl
    d_core = d + 1 - 2 * c
    d_x = [(d + 4 * o) % 16 for o in (1, 2, 3)]
    own = x * 4 + c * 2 + yl
    pair = x * 4 + c * 2 + 1 - yl
    first = x * 4 + c * 2

    def remote(src, dst, sem, device):
        return pltpu.make_async_remote_copy(
            src_ref=src, dst_ref=dst, send_sem=send_sem.at[sem], recv_sem=recv_sem.at[sem],
            device_id=device, device_id_type=MESH,
        )

    def feature(e):
        return (e // 4) * 4 + (e % 2) * 2 + (e // 2) % 2

    def columns(f):
        return pl.ds(pl.multiple_of(f * SHARE, 128), SHARE)

    def wide(i):
        return pl.ds(pl.multiple_of(i * WIDE, 128), WIDE)

    def chunk_rows(k):
        if isinstance(k, int):
            return pl.ds(k * CHUNK, CHUNK)
        return pl.ds(pl.multiple_of(k * CHUNK, CHUNK), CHUNK)

    loads = [
        pltpu.make_async_copy(w_down.at[0], W.at[own, 0], local_sem.at[0]),
        pltpu.make_async_copy(w_up.at[0], W.at[own, 1], local_sem.at[1]),
        pltpu.make_async_copy(stash, st, local_sem.at[2]),
        pltpu.make_async_copy(grad, gr, local_sem.at[3]),
        pltpu.make_async_copy(base, ba, local_sem.at[4]),
    ]
    for load in loads:
        load.start()
    gain_own[...] = gain[...].astype(f32)

    barrier = pltpu.get_barrier_semaphore()
    partners = [(far, d), (z_down, d), (z_up, d), (s, d_pair), (s, d_core), (far, d_pair)]
    partners += [(s, t) for t in d_x]
    for t in partners:
        pl.semaphore_signal(barrier, inc=1, device_id=t, device_id_type=MESH)
    pl.semaphore_wait(barrier, len(partners))

    w_pair = remote(W.at[own], W.at[own], 0, (s, d_pair))
    w_x_own = [remote(W.at[own], W.at[own], 1 + i, (s, t)) for i, t in enumerate(d_x)]
    w_x_pair = [remote(W.at[pair], W.at[pair], 4 + i, (s, t)) for i, t in enumerate(d_x)]

    def group(buf, xs):
        return buf.at[pl.ds(xs * 4 + c * 2, 2)]

    def group_down(xs):
        return W.at[pl.ds(xs * 4 + c * 2, 2), 0]

    x_from = [(x + 4 - o) % 4 for o in range(4)]
    w_core = [remote(group(W, x_from[o]), group(W, x_from[o]), 7 + o, (s, d_core)) for o in range(4)]
    ws_far = remote(group_down(x), group(WS, x), 11, (far, d_pair))
    ws_x = [remote(group(WS, x), group(WS, x), 12 + i, (s, t)) for i, t in enumerate(d_x)]
    ws_core = [remote(group(WS, x_from[o]), group(WS, x_from[o]), 15 + o, (s, d_core)) for o in range(4)]
    gain_copy = remote(gain_own, gain_far, 19, (far, d))
    delta_copy = remote(delta_own, delta_far, 20, (far, d))
    low_copy = remote(low_own, low_far, 21, (far, d))
    part_copy = remote(part_send, part_recv, 22, (s, d_core))
    sum_copy = [remote(sum_send.at[(x + o) % 4], sum_recv.at[o - 1], 22 + o, (s, d_x[o - 1])) for o in (1, 2, 3)]
    cross_copy = remote(cross_send, cross_recv, 26, (far, d_pair))
    pair_copy = remote(pair_send, pair_recv, 27, (s, d_pair))

    def stash_copy(k):
        return remote(stash.at[chunk_rows(k)], sv.at[chunk_rows(k)], 28 + k, (far, d))

    def relay_copy(k):
        return remote(sv.at[chunk_rows(k)], sv.at[chunk_rows(k)], 28 + k, (far, d))

    def z_copy(k):
        return remote(sv.at[chunk_rows(k)], gp.at[chunk_rows(k)], 28 + CHUNKS + k, (z_down, d))

    loads[0].wait()
    loads[1].wait()
    w_pair.start()
    for copy in w_x_own:
        copy.start()
    gain_copy.start()

    @pl.when(s != 8)
    def _():
        for k in range(CHUNKS):
            stash_copy(k).start()

    loads[2].wait()

    def mean_and_inverse(ref, rows, extra=None):
        def add(i, acc):
            return acc + fold(ref[rows, wide(i)].astype(f32))

        zero = jnp.zeros((CHUNK, 128), f32)
        mean = row_sum(lax.fori_loop(0, WIDES, add, zero)) * (1.0 / D)

        def add_square(i, acc):
            centred = ref[rows, wide(i)].astype(f32) - mean
            total = acc[0] + fold(centred * centred)
            if extra is None:
                return (total,)
            return (total, acc[1] + fold(centred * extra[rows, wide(i)]))

        sums = lax.fori_loop(0, WIDES, add_square, (zero,) if extra is None else (zero, zero))
        inverse = lax.rsqrt(row_sum(sums[0]) * (1.0 / D) + norm_eps)
        if extra is None:
            return mean, inverse
        return mean, inverse, row_sum(sums[1]) * (1.0 / D)

    def row_stats(r, carry):
        rows = chunk_rows(r)
        mean, inverse = mean_and_inverse(st, rows)
        b_mean[rows, :] = mean
        inv_row[rows, :] = inverse
        return carry

    lax.fori_loop(0, CHUNKS, row_stats, 0)

    w_pair.wait_recv()
    for copy in w_x_pair:
        copy.start()
    ws_far.start()
    w_core[0].start()

    gain_copy.wait_recv()

    def write_normed(r, carry):
        rows = chunk_rows(r)
        mean, inverse = b_mean[rows, :], inv_row[rows, :]

        def one(i, carry):
            centred = st[rows, wide(i)].astype(f32) - mean
            st[rows, wide(i)] = ((centred * inverse) * gain_far[:, wide(i)]).astype(bf16)
            return carry

        return lax.fori_loop(0, WIDES, one, carry)

    lax.fori_loop(0, CHUNKS, write_normed, 0)

    ws_far.wait_recv()
    for copy in ws_x:
        copy.start()
    ws_core[0].start()

    for o in (1, 3, 2):
        w_x_own[o - 1].wait_recv()
        w_x_pair[o - 1].wait_recv()
        w_core[o].start()
    loads[3].wait()
    loads[4].wait()
    for o in (0, 1, 3, 2):
        w_core[o].wait_recv()

    def add_delta(e, acc):
        return acc + dot_last(gr[:, columns(feature(e))], W[e, 1])

    delta = lax.fori_loop(0, 16, add_delta, jnp.zeros((ROWS, RANK), f32))
    delta_own[...] = jnp.zeros((ROWS, 128), bf16)
    delta_own[:, :RANK] = delta.astype(bf16)
    delta_copy.start()

    def write_b(e, acc):
        cols = columns(feature(e))
        back = jnp.dot(delta_own[:, :RANK], W[e, 0], preferred_element_type=f32)
        value = (ba[:, cols].astype(f32) + back) * gain_own[:, cols]
        b[:, cols] = value
        return acc + fold(value)

    b_sum = lax.fori_loop(0, 16, write_b, jnp.zeros((ROWS, 128), f32))
    b_mean[...] = row_sum(b_sum) * (1.0 / D)

    def grad_chunk(k):
        rows = chunk_rows(k)
        mean, inverse, cross = mean_and_inverse(sv, rows, b)
        first_mean = b_mean[rows, :]
        second_mean = cross * inverse

        def one(i, carry):
            unit = (sv[rows, wide(i)].astype(f32) - mean) * inverse
            value = inverse * (b[rows, wide(i)] - first_mean - unit * second_mean)
            sv[rows, wide(i)] = value.astype(bf16)
            return carry

        lax.fori_loop(0, WIDES, one, 0)

    def step(k):
        @pl.when(s != 0)
        def _():
            stash_copy(k).wait_recv()
            grad_chunk(k)

        @pl.when(s == 8)
        def _():
            relay_copy(k).start()

        @pl.when(jnp.logical_and(s != 0, s != 8))
        def _():
            z_copy(k).start()

        if k > 0:
            relay(k - 1)

    def relay(k):
        @pl.when(s == 0)
        def _():
            relay_copy(k).wait_recv()
            z_copy(k).start()

    step(0)
    step(1)

    for o in (1, 3, 2):
        ws_x[o - 1].wait_recv()
        ws_core[o].start()

    step(2)

    for o in (0, 1, 3, 2):
        ws_core[o].wait_recv()

    def add_low(e, acc):
        return acc + dot_last(st[:, columns(feature(e))], WS[e])

    low = lax.fori_loop(0, 16, add_low, jnp.zeros((ROWS, RANK), f32))
    low_own[...] = jnp.zeros((ROWS, 128), bf16)
    low_own[:, :RANK] = low.astype(bf16)
    low_copy.start()

    step(3)

    delta_copy.wait_recv()
    low_copy.wait_recv()
    delta_t = delta_far[...].astype(f32).T[:RANK].astype(bf16)
    low_t = low_far[...].astype(f32).T[:RANK].astype(bf16)

    def write_parts(j, carry):
        f = (j // 2) * 4 + (j % 2) * 2
        for buf, core in ((part_keep, c), (part_send, 1 - c)):
            cols = columns(f + core)
            one = jnp.dot(delta_t, st[:, cols], preferred_element_type=f32) * (1.0 / TOKENS)
            two = jnp.dot(low_t, gr[:, cols], preferred_element_type=f32) * (1.0 / TOKENS)
            buf[j, 0] = one.astype(bf16)
            buf[j, 1] = two.astype(bf16)
        return carry

    lax.fori_loop(0, 8, write_parts, 0)
    part_copy.start()

    step(4)

    part_copy.wait_recv()

    def add_parts(j, carry):
        total = part_keep[j].astype(f32) + part_recv[j].astype(f32)
        sum_send[j // 2, j % 2] = total.astype(bf16)
        return carry

    lax.fori_loop(0, 8, add_parts, 0)
    for copy in sum_copy:
        copy.start()

    step(5)

    for copy in sum_copy:
        copy.wait_recv()

    def total_of(y, kind):
        total = sum_send[x, y, kind].astype(f32)
        for i in range(3):
            total = total + sum_recv[i, y, kind].astype(f32)
        return total

    for y in range(2):
        cross_send[y] = total_of(y, 0).astype(bf16)
    cross_copy.start()
    pair_send[1] = total_of(1 - yl, 1).astype(bf16)
    kept[...] = total_of(yl, 1)

    step(6)

    cross_copy.wait_recv()
    pair_send[0] = cross_recv[1 - yl]
    pair_copy.start()

    step(7)

    pair_copy.wait_recv()
    g1_out[...] = cross_recv[yl].astype(f32) + pair_recv[0].astype(f32)
    g2_out[...] = kept[...] + pair_recv[1].astype(f32)

    @pl.when(s == 15)
    def _():
        ba[...] = jnp.zeros_like(ba)
        zeros = pltpu.make_async_copy(ba, gp, local_sem.at[5])
        zeros.start()
        zeros.wait()

    relay(CHUNKS - 1)

    sent = [w_pair, *w_x_own, *w_x_pair, *w_core, ws_far, *ws_x, *ws_core]
    sent += [gain_copy, delta_copy, low_copy, part_copy, *sum_copy, cross_copy, pair_copy]
    for copy in sent:
        copy.wait_send()
    for k in range(CHUNKS):
        stash_copy(k).wait_send()

        @pl.when(s != 8)
        def _():
            z_copy(k).wait_send()

        @pl.when(s != 15)
        def _():
            z_copy(k).wait_recv()


def lion(moment, gradient):
    blend = beta_one * moment + (1.0 - beta_one) * gradient
    direction = (blend / (jnp.abs(blend) + lion_delta)).astype(bf16)
    renewed = (beta_two * moment + (1.0 - beta_two) * gradient).astype(bf16)
    return direction, renewed


def shards(stash, grad_in, base_back, gain, w_down, w_up, mom_down, mom_up):
    hbm = pl.BlockSpec(memory_space=pl.ANY)
    vmem = pl.BlockSpec(memory_space=pltpu.VMEM)
    share = (RANK, SHARE)
    upstream, grad_first, grad_second = pl.pallas_call(
        main_kernel,
        out_shape=(
            jax.ShapeDtypeStruct((ROWS, D), bf16),
            jax.ShapeDtypeStruct(share, f32),
            jax.ShapeDtypeStruct(share, f32),
        ),
        in_specs=[hbm, hbm, hbm, vmem, hbm, hbm],
        out_specs=(hbm, vmem, vmem),
        scratch_shapes=[
            pltpu.VMEM((ROWS, D), bf16),
            pltpu.VMEM((ROWS, D), bf16),
            pltpu.VMEM((ROWS, D), bf16),
            pltpu.VMEM((ROWS, D), bf16),
            pltpu.VMEM((ROWS, D), f32),
            pltpu.VMEM((16, 2) + share, bf16),
            pltpu.VMEM((16,) + share, bf16),
            pltpu.VMEM((1, D), f32),
            pltpu.VMEM((1, D), f32),
            pltpu.VMEM((ROWS, 128), bf16),
            pltpu.VMEM((ROWS, 128), bf16),
            pltpu.VMEM((ROWS, 128), bf16),
            pltpu.VMEM((ROWS, 128), bf16),
            pltpu.VMEM((ROWS, 1), f32),
            pltpu.VMEM((ROWS, 1), f32),
            pltpu.VMEM((8, 2) + share, bf16),
            pltpu.VMEM((8, 2) + share, bf16),
            pltpu.VMEM((8, 2) + share, bf16),
            pltpu.VMEM((4, 2, 2) + share, bf16),
            pltpu.VMEM((3, 2, 2) + share, bf16),
            pltpu.VMEM((2,) + share, bf16),
            pltpu.VMEM((2,) + share, bf16),
            pltpu.VMEM((2,) + share, bf16),
            pltpu.VMEM((2,) + share, bf16),
            pltpu.VMEM(share, f32),
            pltpu.SemaphoreType.DMA((6,)),
            pltpu.SemaphoreType.DMA((28 + 2 * CHUNKS,)),
            pltpu.SemaphoreType.DMA((28 + 2 * CHUNKS,)),
        ],
        compiler_params=pltpu.CompilerParams(
            collective_id=0, has_side_effects=True, vmem_limit_bytes=52 * 1024 * 1024
        ),
        cost_estimate=pl.CostEstimate(flops=2 * 5 * ROWS * D * RANK, bytes_accessed=16 * ROWS * D, transcendentals=0),
        name="block",
    )(stash[0], grad_in[0], base_back[0], gain, w_down, w_up)
    step_first, moment_first = lion(mom_down[0].astype(f32), grad_first)
    step_second, moment_second = lion(mom_up[0].astype(f32), grad_second)
    return (
        upstream[None],
        step_first[None],
        step_second[None],
        moment_first[None],
        moment_second[None],
    )


def solution(mesh):
    rows = P("pipe", "dp", None)
    share = P("pipe", None, "dp")
    return jax.shard_map(
        shards,
        mesh=mesh,
        in_specs=(rows, rows, rows, P("pipe", None), share, share, share, share),
        out_specs=(rows, share, share, share, share),
        check_vma=False,
    )
```

time: 265 us -> 193 us (0.73)
  the two profiles are of different devices: /device:TPU:255 before, /device:TPU:1 now
where the time goes in v1:
time: 193 us; the launch traced here: 192 us
  Pallas kernels  185 us (96%)
  local copies, waits for them, and re-layouts  6.41 us (3%)
    pallas_call x1, Pallas kernels, shards(): pl.pallas_call(main_kernel, out_shape=(jax.ShapeDtypeStruct((ROWS, D), bf...  185 us
    unnamed x11, local copies, waits for them, and re-layouts  6.41 us

profile of v1, /device:TPU:1, one launch (start us, length us, event | category | flops | bytes accessed | tf_op | source)
XLA Modules:
  0.0 192.5 jit_solution(9824713707128628814)
XLA Ops:
  0.6 0.0 copy-start
  0.6 0.9 copy-done
  1.5 0.0 copy-start.1
  1.5 0.9 copy-done.1
  2.4 0.0 copy-start.2
  2.4 0.8 copy-done.2
  3.2 0.0 copy-start.3
  3.2 0.0 copy-start.4
  3.2 184.5 %block.1 = (bf16[128,12288]{1,0:T(8,128)(2,1)}, f32[64,768]{1,0:T(8,128)S(1)}, f32[64,768]{1,0:T(8,128)S(1)}) custom-call(bf16[128,12288]{1,0:T(8,128)(2,1)} %bitcast.45, bf16[128,12288]{1,0:T(8,128)(2,1)} %bitcast.46, bf16[128,12288]{1,0:T(8,128)(2,1)} %bitcast.47, bf16[1,12288]{1,0:T(2,128)(2,1)S(1)} %copy-done.2, bf16[1,64,768]{2,1,0:T(8,128)(2,1)S(1)} %copy-done, ...), custom_call_target="tpu_custom_call" | custom-call | flops 1006632960 | bytes 25165824 | tf_op jit(solution)/shard_map/block/pallas_call | solution.py:393
  187.8 0.0 copy-done.3
  187.8 0.0 copy-done.4
  187.8 0.9 fusion.10
  188.7 3.8 %copy.14 = bf16[1,128,12288]{2,1,0:T(8,128)(2,1)} copy(bf16[1,128,12288]{2,1,0:T(8,128)(2,1)} %bitcast.44) | data formatting | bytes 6291456
Async XLA Ops:
  0.6 0.9 copy-start
  1.5 0.9 copy-start.1
  2.4 0.8 copy-start.2
  3.2 184.6 %copy-start.3 = (bf16[1,64,768]{2,1,0:T(8,128)(2,1)S(1)}, bf16[1,64,768]{2,1,0:T(8,128)(2,1)}, u32[]{:S(2)}) copy-start(bf16[1,64,768]{2,1,0:T(8,128)(2,1)} %param.15) | copy-start | bytes 294916
  3.2 184.6 %copy-start.4 = (bf16[1,64,768]{2,1,0:T(8,128)(2,1)S(1)}, bf16[1,64,768]{2,1,0:T(8,128)(2,1)}, u32[]{:S(2)}) copy-start(bf16[1,64,768]{2,1,0:T(8,128)(2,1)} %param.14) | copy-start | bytes 294916

commit v2 on v1

v2 whole, which is shorter than its diff:
```python
import functools

import jax
import jax.numpy as jnp
from jax import lax
from jax.experimental import pallas as pl
from jax.experimental.pallas import tpu as pltpu
from jax.sharding import PartitionSpec as P

norm_eps = 1e-05
beta_one = 0.9
beta_two = 0.99
lion_delta = 0.003

D = 12288
RANK = 64
ROWS = 128
TOKENS = 2048
SHARE = D // 16
CHUNK = 16
CHUNKS = ROWS // CHUNK
WIDE = 1536
WIDES = D // WIDE
PARTS = 4
PART = D // PARTS
CORE = 48 + CHUNKS * PARTS
SEMS = CORE + 8
MESH = pl.DeviceIdType.MESH
VMEM_LIMIT = 63 * 1024 * 1024
f32 = jnp.float32
bf16 = jnp.bfloat16

contract_last = (((1,), (1,)), ((), ()))


def dot_last(a, b):
    return lax.dot_general(a, b, contract_last, preferred_element_type=f32)


def fold(v):
    parts = [v[:, i : i + 128] for i in range(0, v.shape[1], 128)]
    while len(parts) > 1:
        half = [a + b for a, b in zip(parts[::2], parts[1::2])]
        if len(parts) % 2:
            half.append(parts[-1])
        parts = half
    return parts[0]


def row_sum(acc):
    return jnp.sum(acc, axis=1, keepdims=True)


def lion(moment, gradient):
    blend = beta_one * moment + (1.0 - beta_one) * gradient
    direction = (blend / (jnp.abs(blend) + lion_delta)).astype(bf16)
    renewed = (beta_two * moment + (1.0 - beta_two) * gradient).astype(bf16)
    return direction, renewed


def main_kernel(
    stash, grad, base, gain, w_down, w_up, mom_down, mom_up,
    gp, step1, step2, new1, new2,
    m1, m2,    gain_in, gain_land, st, sv, gr, ba, b, W, WS, gain_own, gain_far,
    delta_own, delta_far, low_own, low_far, b_mean, mean_row, inv_row,
    part_send, part_keep, part_recv, sum_send, sum_recv,
    pair_send, pair_recv, kept, final_send, final_recv,
    local_sem, send_sem, recv_sem,
):
    s = lax.axis_index("pipe")
    d = lax.axis_index("dp")
    x, yl, c = d // 4, (d // 2) % 2, d % 2
    far = (s + 8) % 16
    z = s % 8
    z_down = s - z + (z + 7) % 8
    z_up = s - z + (z + 1) % 8
    d_pair = d + 2 - 4 * yl
    d_core = d + 1 - 2 * c
    d_x = [(d + 4 * o) % 16 for o in (1, 2, 3)]
    own = x * 4 + c * 2 + yl
    pair = x * 4 + c * 2 + 1 - yl
    first = x * 4 + c * 2

    def remote(src, dst, sem, device):
        return pltpu.make_async_remote_copy(
            src_ref=src, dst_ref=dst, send_sem=send_sem.at[sem], recv_sem=recv_sem.at[sem],
            device_id=device, device_id_type=MESH,
        )

    def feature(e):
        return (e // 4) * 4 + (e % 2) * 2 + (e // 2) % 2

    def columns(f):
        return pl.ds(pl.multiple_of(f * SHARE, 128), SHARE)

    def wide(i):
        return pl.ds(pl.multiple_of(i * WIDE, 128), WIDE)

    def chunk_rows(k):
        if isinstance(k, int):
            return pl.ds(k * CHUNK, CHUNK)
        return pl.ds(pl.multiple_of(k * CHUNK, CHUNK), CHUNK)

    loads = [
        pltpu.make_async_copy(w_down.at[0], W.at[own, 0], local_sem.at[0]),
        pltpu.make_async_copy(w_up.at[0], W.at[own, 1], local_sem.at[1]),
        pltpu.make_async_copy(stash, st, local_sem.at[2]),
        pltpu.make_async_copy(grad, gr, local_sem.at[3]),
        pltpu.make_async_copy(base, ba, local_sem.at[4]),
        pltpu.make_async_copy(gain, gain_in, local_sem.at[5]),
        pltpu.make_async_copy(mom_down.at[0], m1, local_sem.at[6]),
        pltpu.make_async_copy(mom_up.at[0], m2, local_sem.at[7]),
    ]
    for i in (0, 1, 5, 2, 3, 4, 6, 7):
        loads[i].start()

    barrier = pltpu.get_barrier_semaphore()
    partners = [(far, d), (z_down, d), (z_up, d), (s, d_pair), (s, d_core), (far, d_pair), (15 - s, d)]
    partners += [(s, t) for t in d_x]
    for t in partners:
        pl.semaphore_signal(barrier, inc=1, device_id=t, device_id_type=MESH)
    pl.semaphore_wait(barrier, len(partners))

    w_pair = remote(W.at[own], W.at[own], 0, (s, d_pair))
    right, left = d_x[0], d_x[2]
    kinds = (yl, 1 - yl)

    def slot_of(o, kind):
        return ((x + 4 - o) % 4) * 4 + c * 2 + kinds[kind]

    w_right = [remote(W.at[slot_of(0, i)], W.at[slot_of(0, i)], 1 + i, (s, right)) for i in range(2)]
    w_left = [remote(W.at[slot_of(0, i)], W.at[slot_of(0, i)], 3 + i, (s, left)) for i in range(2)]
    w_on_right = [remote(W.at[slot_of(1, i), 0], W.at[slot_of(1, i), 0], 44 + i, (s, right)) for i in range(2)]
    w_on_left = [remote(W.at[slot_of(3, i), 1], W.at[slot_of(3, i), 1], 46 + i, (s, left)) for i in range(2)]

    def group(xs):
        return WS.at[pl.ds(xs * 4 + c * 2, 2)]

    def core_copy(o, kind):
        slot = W.at[slot_of(o, kind)]
        return remote(slot, slot, CORE + 2 * o + kind, (s, d_core))

    x_from = [(x + 4 - o) % 4 for o in range(4)]
    w_core = [[core_copy(o, kind) for kind in range(2)] for o in range(4)]
    ws_far = remote(W.at[own, 0], WS.at[own], 11, (far, d))
    ws_cross = remote(W.at[own, 0], WS.at[own], 26, (far, d_pair))
    ws_x = [remote(group(x), group(x), 12 + i, (s, t)) for i, t in enumerate(d_x)]
    ws_core = [remote(group(x_from[o]), group(x_from[o]), 15 + o, (s, d_core)) for o in range(4)]
    gain_copy = remote(gain_in, gain_land, 19, (far, d_pair))
    delta_copy = remote(delta_own, delta_far, 20, (far, d))
    low_copy = remote(low_own, low_far, 21, (far, d))
    part_copy = remote(part_send, part_recv, 22, (s, d_core))
    sum_copy = [remote(sum_send.at[(x + o) % 4], sum_recv.at[o - 1], 22 + o, (s, d_x[o - 1])) for o in (1, 2, 3)]
    final_copy = remote(final_send, final_recv, 5, (far, d))
    pair_copy = remote(pair_send, pair_recv, 27, (s, d_pair))

    def stash_copy(k):
        return remote(stash.at[chunk_rows(k)], sv.at[chunk_rows(k)], 28 + k, (far, d))

    def relay_part(k, i):
        part = sv.at[chunk_rows(k), pl.ds(i * PART, PART)]
        return remote(part, part, 48 + k * PARTS + i, (far, d))

    def direct_copy(k):
        return remote(sv.at[chunk_rows(k)], gp.at[chunk_rows(k)], 28 + CHUNKS + k, (15 - s, d))

    def z_part(k, i):
        part = (chunk_rows(k), pl.ds(i * PART, PART))
        return remote(sv.at[part], gp.at[part], 28 + CHUNKS + k, (z_down, d))

    def z_copy(k):
        return remote(sv.at[chunk_rows(k)], gp.at[chunk_rows(k)], 28 + CHUNKS + k, (z_down, d))

    loads[0].wait()
    loads[1].wait()
    w_pair.start()
    w_right[0].start()
    w_left[0].start()
    ws_cross.start()
    ws_far.start()
    w_core[0][0].start()
    loads[5].wait()
    gain_copy.start()

    def pump(k):
        if k < 3:
            @pl.when(s != 8)
            def _():
                stash_copy(k).start()
        else:
            @pl.when(jnp.logical_and(s != 8, s != 0))
            def _():
                stash_copy(k).start()

    def pump_rest():
        @pl.when(s == 0)
        def _():
            for k in range(3, CHUNKS):
                stash_copy(k).start()

    pump(0)
    gain_own[...] = gain_in[...].astype(f32)

    loads[2].wait()

    def mean_and_inverse(ref, rows, extra=None):
        def add(i, acc):
            return acc + fold(ref[rows, wide(i)].astype(f32))

        zero = jnp.zeros((CHUNK, 128), f32)
        mean = row_sum(lax.fori_loop(0, WIDES, add, zero)) * (1.0 / D)

        def add_square(i, acc):
            centred = ref[rows, wide(i)].astype(f32) - mean
            total = acc[0] + fold(centred * centred)
            if extra is None:
                return (total,)
            return (total, acc[1] + fold(centred * extra[rows, wide(i)]))

        sums = lax.fori_loop(0, WIDES, add_square, (zero,) if extra is None else (zero, zero))
        inverse = lax.rsqrt(row_sum(sums[0]) * (1.0 / D) + norm_eps)
        if extra is None:
            return mean, inverse
        return mean, inverse, row_sum(sums[1]) * (1.0 / D)

    def row_stats(r, carry):
        rows = chunk_rows(r)
        mean, inverse = mean_and_inverse(st, rows)
        mean_row[rows, :] = mean
        inv_row[rows, :] = inverse
        return carry

    lax.fori_loop(0, CHUNKS, row_stats, 0)

    w_pair.wait_recv()
    w_right[1].start()
    w_left[1].start()
    w_core[0][1].start()
    pump(1)

    def pass_on(i):
        w_right[i].wait_recv()
        w_on_right[i].start()
        w_core[1][i].start()
        w_left[i].wait_recv()
        w_on_left[i].start()
        w_core[3][i].start()

    def end_group(i):
        w_on_right[i].wait_recv()
        w_on_left[i].wait_recv()
        w_core[2][i].start()

    def add_delta(o, acc):
        e = x_from[o] * 4
        for i in range(4):
            acc = acc + dot_last(gr[:, columns(feature(e + i))], W[e + i, 1])
        return acc

    def group_ready(o):
        w_core[o][0].wait_recv()
        w_core[o][1].wait_recv()

    def write_normed(r, carry):
        rows = chunk_rows(r)
        mean, inverse = mean_row[rows, :], inv_row[rows, :]

        def one(i, carry):
            centred = st[rows, wide(i)].astype(f32) - mean
            st[rows, wide(i)] = ((centred * inverse) * gain_far[:, wide(i)]).astype(bf16)
            return carry

        return lax.fori_loop(0, WIDES, one, carry)

    pass_on(0)
    loads[3].wait()
    group_ready(0)
    delta = add_delta(0, jnp.zeros((ROWS, RANK), f32))
    pass_on(1)
    gain_copy.wait_recv()
    gain_far[...] = gain_land[...].astype(f32)
    group_ready(1)
    delta = add_delta(1, delta)
    group_ready(3)
    delta = add_delta(3, delta)
    end_group(0)
    lax.fori_loop(0, 2, write_normed, 0)
    end_group(1)
    ws_far.wait_recv()
    ws_cross.wait_recv()
    for copy in ws_x:
        copy.start()
    ws_core[0].start()
    group_ready(2)
    delta = add_delta(2, delta)
    delta_own[...] = jnp.zeros((ROWS, 128), bf16)
    delta_own[:, :RANK] = delta.astype(bf16)
    delta_copy.start()
    pump(2)

    def fill_b(start, count):
        rows = pl.ds(start, count)

        def write_b(g, acc):
            for i in range(4):
                e = g * 4 + i
                cols = columns(feature(e))
                back = jnp.dot(delta_own[rows, :RANK], W[e, 0], preferred_element_type=f32)
                value = (ba[rows, cols].astype(f32) + back) * gain_own[:, cols]
                b[rows, cols] = value
                acc = acc + fold(value)
            return acc

        b_sum = lax.fori_loop(0, 4, write_b, jnp.zeros((count, 128), f32))
        b_mean[rows, :] = row_sum(b_sum) * (1.0 / D)

    loads[4].wait()
    fill_b(0, 2 * CHUNK)

    def grad_chunk(k):
        rows = chunk_rows(k)
        mean, inverse, cross = mean_and_inverse(sv, rows, b)
        first_mean = b_mean[rows, :]
        second_mean = cross * inverse

        def one(i, carry):
            unit = (sv[rows, wide(i)].astype(f32) - mean) * inverse
            value = inverse * (b[rows, wide(i)] - first_mean - unit * second_mean)
            sv[rows, wide(i)] = value.astype(bf16)
            return carry

        lax.fori_loop(0, WIDES, one, 0)

    def step(k):
        @pl.when(s != 0)
        def _():
            stash_copy(k).wait_recv()
            grad_chunk(k)

        @pl.when(s == 8)
        def _():
            if k == CHUNKS - 1:
                direct_copy(k).start()
            else:
                for i in range(PARTS):
                    relay_part(k, i).start()

        @pl.when(jnp.logical_and(s != 0, s != 8))
        def _():
            z_copy(k).start()

        if k > 0:
            relay(k - 1)

    def relay(k):
        @pl.when(s == 0)
        def _():
            for i in range(PARTS):
                relay_part(k, i).wait_recv()
                z_part(k, i).start()

    step(0)
    fill_b(2 * CHUNK, ROWS - 2 * CHUNK)
    lax.fori_loop(2, CHUNKS, write_normed, 0)
    step(1)

    for o in (1, 3, 2):
        ws_x[o - 1].wait_recv()
        ws_core[o].start()
    for o in (0, 1, 3, 2):
        ws_core[o].wait_recv()

    def add_low(g, acc):
        for i in range(4):
            e = g * 4 + i
            acc = acc + dot_last(st[:, columns(feature(e))], WS[e])
        return acc

    low = lax.fori_loop(0, 4, add_low, jnp.zeros((ROWS, RANK), f32))
    low_own[...] = jnp.zeros((ROWS, 128), bf16)
    low_own[:, :RANK] = low.astype(bf16)
    low_copy.start()
    pump(3)
    pump_rest()
    step(2)
    pump(4)

    delta_copy.wait_recv()
    low_copy.wait_recv()
    delta_t = delta_far[...].astype(f32).T[:RANK].astype(bf16)
    low_t = low_far[...].astype(f32).T[:RANK].astype(bf16)

    def write_parts(j, carry):
        f = (j // 2) * 4 + (j % 2) * 2
        for buf, core in ((part_keep, c), (part_send, 1 - c)):
            cols = columns(f + core)
            one = jnp.dot(delta_t, st[:, cols], preferred_element_type=f32) * (1.0 / TOKENS)
            two = jnp.dot(low_t, gr[:, cols], preferred_element_type=f32) * (1.0 / TOKENS)
            buf[j, 0] = one.astype(bf16)
            buf[j, 1] = two.astype(bf16)
        return carry

    lax.fori_loop(0, 8, write_parts, 0)
    part_copy.start()
    step(3)
    pump(5)

    part_copy.wait_recv()

    def add_parts(j, carry):
        total = part_keep[j].astype(f32) + part_recv[j].astype(f32)
        sum_send[j // 2, j % 2] = total.astype(bf16)
        return carry

    lax.fori_loop(0, 8, add_parts, 0)
    for copy in sum_copy:
        copy.start()

    step(4)
    pump(6)
    step(5)
    pump(7)

    for copy in sum_copy:
        copy.wait_recv()

    def total_of(y, kind):
        total = sum_send[x, y, kind].astype(f32)
        for i in range(3):
            total = total + sum_recv[i, y, kind].astype(f32)
        return total

    for kind in range(2):
        pair_send[kind] = total_of(1 - yl, kind).astype(bf16)
        kept[kind] = total_of(yl, kind)
    pair_copy.start()

    step(6)
    step(7)

    pair_copy.wait_recv()
    final_send[...] = (kept[0] + pair_recv[0].astype(f32)).astype(bf16)
    final_copy.start()
    loads[7].wait()
    step2[...], new2[...] = lion(m2[...].astype(f32), kept[1] + pair_recv[1].astype(f32))
    final_copy.wait_recv()
    loads[6].wait()
    step1[...], new1[...] = lion(m1[...].astype(f32), final_recv[...].astype(f32))

    @pl.when(s == 15)
    def _():
        ba[...] = jnp.zeros_like(ba)
        zeros = pltpu.make_async_copy(ba, gp, local_sem.at[8])
        zeros.start()
        zeros.wait()

    sent = [w_pair, *w_right, *w_left, *w_on_right, *w_on_left, ws_far, ws_cross, *ws_x, *ws_core]
    sent += [copy for pair_of in w_core for copy in pair_of]
    sent += [gain_copy, delta_copy, low_copy, part_copy, *sum_copy, pair_copy, final_copy]
    for copy in sent:
        copy.wait_send()
    for k in range(CHUNKS):
        @pl.when(s != 8)
        def _():
            stash_copy(k).wait_send()
            if k < CHUNKS - 1:
                z_copy(k).wait_send()

        @pl.when(s == 8)
        def _():
            if k < CHUNKS - 1:
                for i in range(PARTS):
                    relay_part(k, i).wait_send()

        if k == CHUNKS - 1:
            @pl.when(s != 0)
            def _():
                z_copy(k).wait_send()

        @pl.when(s != 15)
        def _():
            z_copy(k).wait_recv()


def finish_kernel(rows, a, b, c, d, rows_out, a_out, b_out, c_out, d_out, held, small, sem_in, sem_out):
    moves = [(a, small.at[0], a_out), (b, small.at[1], b_out), (c, small.at[2], c_out), (d, small.at[3], d_out)]
    for k in range(CHUNKS):
        part = pl.ds(k * CHUNK, CHUNK)
        moves.append((rows.at[part], held.at[part], rows_out.at[part]))
    into = [pltpu.make_async_copy(m[0], m[1], sem_in.at[i]) for i, m in enumerate(moves)]
    out = [pltpu.make_async_copy(m[1], m[2], sem_out.at[i]) for i, m in enumerate(moves)]
    for copy in into:
        copy.start()
    for first, second in zip(into, out):
        first.wait()
        second.start()
    for copy in out:
        copy.wait()


def shards(stash, grad_in, base_back, gain, w_down, w_up, mom_down, mom_up):
    hbm = pl.BlockSpec(memory_space=pltpu.HBM)
    vmem = pl.BlockSpec(memory_space=pltpu.VMEM)
    share = (RANK, SHARE)
    maps = jax.ShapeDtypeStruct(share, bf16)
    shapes = (jax.ShapeDtypeStruct((ROWS, D), bf16), maps, maps, maps, maps)
    outs = pl.pallas_call(
        main_kernel,
        out_shape=shapes,
        in_specs=[hbm] * 8,
        out_specs=(hbm, vmem, vmem, vmem, vmem),
        scratch_shapes=[
            pltpu.VMEM(share, bf16),
            pltpu.VMEM(share, bf16),
            pltpu.VMEM((1, D), bf16),
            pltpu.VMEM((1, D), bf16),
            pltpu.VMEM((ROWS, D), bf16),
            pltpu.VMEM((ROWS, D), bf16),
            pltpu.VMEM((ROWS, D), bf16),
            pltpu.VMEM((ROWS, D), bf16),
            pltpu.VMEM((ROWS, D), f32),
            pltpu.VMEM((16, 2) + share, bf16),
            pltpu.VMEM((16,) + share, bf16),
            pltpu.VMEM((1, D), f32),
            pltpu.VMEM((1, D), f32),
            pltpu.VMEM((ROWS, 128), bf16),
            pltpu.VMEM((ROWS, 128), bf16),
            pltpu.VMEM((ROWS, 128), bf16),
            pltpu.VMEM((ROWS, 128), bf16),
            pltpu.VMEM((ROWS, 1), f32),
            pltpu.VMEM((ROWS, 1), f32),
            pltpu.VMEM((ROWS, 1), f32),
            pltpu.VMEM((8, 2) + share, bf16),
            pltpu.VMEM((8, 2) + share, bf16),
            pltpu.VMEM((8, 2) + share, bf16),
            pltpu.VMEM((4, 2, 2) + share, bf16),
            pltpu.VMEM((3, 2, 2) + share, bf16),
            pltpu.VMEM((2,) + share, bf16),
            pltpu.VMEM((2,) + share, bf16),
            pltpu.VMEM((2,) + share, f32),
            pltpu.VMEM(share, bf16),
            pltpu.VMEM(share, bf16),
            pltpu.SemaphoreType.DMA((9,)),
            pltpu.SemaphoreType.DMA((SEMS,)),
            pltpu.SemaphoreType.DMA((SEMS,)),
        ],
        compiler_params=pltpu.CompilerParams(
            collective_id=0, has_side_effects=True, vmem_limit_bytes=VMEM_LIMIT
        ),
        cost_estimate=pl.CostEstimate(flops=2 * 5 * ROWS * D * RANK, bytes_accessed=16 * ROWS * D, transcendentals=0),
        name="block",
    )(stash[0], grad_in[0], base_back[0], gain, w_down, w_up, mom_down, mom_up)
    outs = pl.pallas_call(
        finish_kernel,
        out_shape=shapes,
        in_specs=[hbm] * 5,
        out_specs=(hbm,) * 5,
        scratch_shapes=[
            pltpu.VMEM((ROWS, D), bf16),
            pltpu.VMEM((4,) + share, bf16),
            pltpu.SemaphoreType.DMA((CHUNKS + 4,)),
            pltpu.SemaphoreType.DMA((CHUNKS + 4,)),
        ],
        compiler_params=pltpu.CompilerParams(vmem_limit_bytes=VMEM_LIMIT),
        name="finish",
    )(*outs)
    return tuple(out[None] for out in outs)


def solution(mesh):
    rows = P("pipe", "dp", None)
    share = P("pipe", None, "dp")
    return jax.shard_map(
        shards,
        mesh=mesh,
        in_specs=(rows, rows, rows, P("pipe", None), share, share, share, share),
        out_specs=(rows, share, share, share, share),
        check_vma=False,
    )
```

time: 193 us -> 109 us (0.56)
  Pallas kernels: 185 us -> 108 us
  local copies, waits for them, and re-layouts: 6.41 us -> 0 us
    pallas_call x1 -> x2, Pallas kernels: 185 us -> 108 us  [the longest x1 105 us: shards(): pl.pallas_call(main_kernel, out_shape=shapes, in_specs=[hbm] * 8, out_spe...]
    unnamed x11 -> x0, local copies, waits for them, and re-layouts: 6.41 us -> none
where the time goes in v2:
time: 109 us
  Pallas kernels  108 us (99%)
    pallas_call x1, Pallas kernels, shards(): pl.pallas_call(main_kernel, out_shape=shapes, in_specs=[hbm] * 8, out_spe...  105 us
    pallas_call x1, Pallas kernels, shards(): pl.pallas_call(finish_kernel, out_shape=shapes, in_specs=[hbm] * 5, out_s...  3.29 us

profile of v2, /device:TPU:1, one launch (start us, length us, event | category | flops | bytes accessed | tf_op | source)
XLA Modules:
  0.0 108.5 jit_solution(10355531117455182720)
XLA Ops:
  0.6 104.6 %block.1 = (bf16[128,12288]{1,0:T(8,128)(2,1)}, bf16[64,768]{1,0:T(8,128)(2,1)}, bf16[64,768]{1,0:T(8,128)(2,1)}, bf16[64,768]{1,0:T(8,128)(2,1)}, bf16[64,768]{1,0:T(8,128)(2,1)}) custom-call(bf16[128,12288]{1,0:T(8,128)(2,1)} %bitcast.8, bf16[128,12288]{1,0:T(8,128)(2,1)} %bitcast.9, bf16[128,12288]{1,0:T(8,128)(2,1)} %bitcast.10, bf16[1,12288]{1,0:T(2,128)(2,1)} %gain.1, ...), custom_call_target="tpu_custom_call" | custom-call | flops 1006632960 | bytes 25165824 | tf_op jit(solution)/shard_map/block/pallas_call | solution.py:507
  105.2 3.3 %finish.1 = (bf16[128,12288]{1,0:T(8,128)(2,1)}, bf16[64,768]{1,0:T(8,128)(2,1)}, bf16[64,768]{1,0:T(8,128)(2,1)}, bf16[64,768]{1,0:T(8,128)(2,1)}, bf16[64,768]{1,0:T(8,128)(2,1)}) custom-call(bf16[128,12288]{1,0:T(8,128)(2,1)} %get-tuple-element.15.rows, bf16[64,768]{1,0:T(8,128)(2,1)} %get-tuple-element.16.a, bf16[64,768]{1,0:T(8,128)(2,1)} %get-tuple-element.17.b, ...), custom_call_target="tpu_custom_call" | custom-call | tf_op jit(solution)/shard_map/finish/pallas_call | solution.py:553

commit v3 on v2

--- a/solution.py
+++ b/solution.py
@@ -21,10 +21,9 @@
 CHUNKS = ROWS // CHUNK
 WIDE = 1536
 WIDES = D // WIDE
-PARTS = 4
-PART = D // PARTS
-CORE = 48 + CHUNKS * PARTS
-SEMS = CORE + 8
+CORE = 48
+HALF = CORE + 8
+SEMS = HALF + 11
 MESH = pl.DeviceIdType.MESH
 VMEM_LIMIT = 63 * 1024 * 1024
 f32 = jnp.float32
@@ -61,16 +60,17 @@
 def main_kernel(
     stash, grad, base, gain, w_down, w_up, mom_down, mom_up,
     gp, step1, step2, new1, new2,
-    m1, m2,    gain_in, gain_land, st, sv, gr, ba, b, W, WS, gain_own, gain_far,
-    delta_own, delta_far, low_own, low_far, b_mean, mean_row, inv_row,
+    results,    m1, m2,    gain_in, gain_land, st, sv, gr, ba, b, W, WS, gain_own, gain_far,
+    delta_sum, delta_own, delta_far, low_own, low_far, b_mean, mean_row, inv_row,
     part_send, part_keep, part_recv, sum_send, sum_recv,
-    pair_send, pair_recv, kept, final_send, final_recv,
+    total_send, total_recv, kept,
     local_sem, send_sem, recv_sem,
 ):
     s = lax.axis_index("pipe")
     d = lax.axis_index("dp")
     x, yl, c = d // 4, (d // 2) % 2, d % 2
     far = (s + 8) % 16
+    with_down = jnp.logical_and(s != 0, s != 8)
     z = s % 8
     z_down = s - z + (z + 7) % 8
     z_up = s - z + (z + 1) % 8
@@ -104,32 +104,40 @@
     loads = [
         pltpu.make_async_copy(w_down.at[0], W.at[own, 0], local_sem.at[0]),
         pltpu.make_async_copy(w_up.at[0], W.at[own, 1], local_sem.at[1]),
+        pltpu.make_async_copy(gain, gain_in, local_sem.at[5]),
         pltpu.make_async_copy(stash, st, local_sem.at[2]),
         pltpu.make_async_copy(grad, gr, local_sem.at[3]),
-        pltpu.make_async_copy(base, ba, local_sem.at[4]),
-        pltpu.make_async_copy(gain, gain_in, local_sem.at[5]),
         pltpu.make_async_copy(mom_down.at[0], m1, local_sem.at[6]),
         pltpu.make_async_copy(mom_up.at[0], m2, local_sem.at[7]),
     ]
-    for i in (0, 1, 5, 2, 3, 4, 6, 7):
-        loads[i].start()
+    for load in loads:
+        load.start()
+
+    base_load = pltpu.make_async_copy(base, ba, local_sem.at[4])
+    saved_load = pltpu.make_async_copy(stash, sv, local_sem.at[4])
+    pl.when(s != 0)(base_load.start)
+    pl.when(s == 0)(saved_load.start)
 
     barrier = pltpu.get_barrier_semaphore()
-    partners = [(far, d), (z_down, d), (z_up, d), (s, d_pair), (s, d_core), (far, d_pair), (15 - s, d)]
+    partners = [(far, d), (z_down, d), (z_up, d), (s, d_pair), (s, d_core), (far, d_pair)]
     partners += [(s, t) for t in d_x]
     for t in partners:
         pl.semaphore_signal(barrier, inc=1, device_id=t, device_id_type=MESH)
     pl.semaphore_wait(barrier, len(partners))
 
-    w_pair = remote(W.at[own], W.at[own], 0, (s, d_pair))
+    w_pair = [remote(W.at[own, j], W.at[own, j], (0, HALF + 8)[j], (s, d_pair)) for j in range(2)]
     right, left = d_x[0], d_x[2]
     kinds = (yl, 1 - yl)
 
     def slot_of(o, kind):
         return ((x + 4 - o) % 4) * 4 + c * 2 + kinds[kind]
 
-    w_right = [remote(W.at[slot_of(0, i)], W.at[slot_of(0, i)], 1 + i, (s, right)) for i in range(2)]
-    w_left = [remote(W.at[slot_of(0, i)], W.at[slot_of(0, i)], 3 + i, (s, left)) for i in range(2)]
+    def half_to(i, j, sem, t):
+        half = W.at[slot_of(0, i), j]
+        return remote(half, half, HALF + sem + 2 * i + j, (s, t))
+
+    w_right = [[half_to(i, j, 0, right) for j in range(2)] for i in range(2)]
+    w_left = [[half_to(i, j, 4, left) for j in range(2)] for i in range(2)]
     w_on_right = [remote(W.at[slot_of(1, i), 0], W.at[slot_of(1, i), 0], 44 + i, (s, right)) for i in range(2)]
     w_on_left = [remote(W.at[slot_of(3, i), 1], W.at[slot_of(3, i), 1], 46 + i, (s, left)) for i in range(2)]
 
@@ -151,57 +159,48 @@
     low_copy = remote(low_own, low_far, 21, (far, d))
     part_copy = remote(part_send, part_recv, 22, (s, d_core))
     sum_copy = [remote(sum_send.at[(x + o) % 4], sum_recv.at[o - 1], 22 + o, (s, d_x[o - 1])) for o in (1, 2, 3)]
-    final_copy = remote(final_send, final_recv, 5, (far, d))
-    pair_copy = remote(pair_send, pair_recv, 27, (s, d_pair))
+    total_to = [(far, d), (far, d_pair), (s, d_pair)]
+    total_copy = [remote(total_send.at[i], total_recv.at[i], (5, 6, 27)[i], to) for i, to in enumerate(total_to)]
 
     def stash_copy(k):
         return remote(stash.at[chunk_rows(k)], sv.at[chunk_rows(k)], 28 + k, (far, d))
 
-    def relay_part(k, i):
-        part = sv.at[chunk_rows(k), pl.ds(i * PART, PART)]
-        return remote(part, part, 48 + k * PARTS + i, (far, d))
-
-    def direct_copy(k):
-        return remote(sv.at[chunk_rows(k)], gp.at[chunk_rows(k)], 28 + CHUNKS + k, (15 - s, d))
-
-    def z_part(k, i):
-        part = (chunk_rows(k), pl.ds(i * PART, PART))
-        return remote(sv.at[part], gp.at[part], 28 + CHUNKS + k, (z_down, d))
+    def base_copy(k):
+        return remote(base.at[chunk_rows(k)], ba.at[chunk_rows(k)], 28 + k, (far, d))
+
+    def base_half(j):
+        half = (chunk_rows(1), pl.ds(j * (D // 2), D // 2))
+        return remote(base.at[half], ba.at[half], HALF + 9 + j, (far, d))
 
     def z_copy(k):
         return remote(sv.at[chunk_rows(k)], gp.at[chunk_rows(k)], 28 + CHUNKS + k, (z_down, d))
 
     loads[0].wait()
     loads[1].wait()
-    w_pair.start()
-    w_right[0].start()
-    w_left[0].start()
+    pl.when(s == 8)(ws_far.start)
+    w_pair[0].start()
+    w_pair[1].start()
+    pl.when(with_down)(w_right[0][0].start)
+    w_left[0][1].start()
+    w_right[0][1].start()
+    pl.when(with_down)(w_left[0][0].start)
+    pl.when(s != 8)(ws_far.start)
+    w_core[0][0].start()
+    loads[2].wait()
+    gain_copy.start()
     ws_cross.start()
-    ws_far.start()
-    w_core[0][0].start()
-    loads[5].wait()
-    gain_copy.start()
 
     def pump(k):
-        if k < 3:
-            @pl.when(s != 8)
-            def _():
-                stash_copy(k).start()
-        else:
-            @pl.when(jnp.logical_and(s != 8, s != 0))
-            def _():
-                stash_copy(k).start()
-
-    def pump_rest():
-        @pl.when(s == 0)
-        def _():
-            for k in range(3, CHUNKS):
-                stash_copy(k).start()
+        @pl.when(jnp.logical_and(s != 0, s != 8))
+        def _():
+            stash_copy(k).start()
+
+        pl.when(s == 8)(base_half(0).start if k == 1 else base_copy(k).start)
 
     pump(0)
     gain_own[...] = gain_in[...].astype(f32)
 
-    loads[2].wait()
+    loads[3].wait()
 
     def mean_and_inverse(ref, rows, extra=None):
         def add(i, acc):
@@ -232,22 +231,21 @@
 
     lax.fori_loop(0, CHUNKS, row_stats, 0)
 
-    w_pair.wait_recv()
-    w_right[1].start()
-    w_left[1].start()
-    w_core[0][1].start()
-    pump(1)
-
     def pass_on(i):
-        w_right[i].wait_recv()
-        w_on_right[i].start()
+        @pl.when(with_down)
+        def _():
+            w_right[i][0].wait_recv()
+            w_on_right[i].start()
+
+        w_left[i][1].wait_recv()
+        w_on_left[i].start()
+        w_right[i][1].wait_recv()
         w_core[1][i].start()
-        w_left[i].wait_recv()
-        w_on_left[i].start()
+        pl.when(with_down)(w_left[i][0].wait_recv)
         w_core[3][i].start()
 
     def end_group(i):
-        w_on_right[i].wait_recv()
+        pl.when(with_down)(w_on_right[i].wait_recv)
         w_on_left[i].wait_recv()
         w_core[2][i].start()
 
@@ -272,30 +270,60 @@
 
         return lax.fori_loop(0, WIDES, one, carry)
 
+    def pair_arrived():
+        w_pair[0].wait_recv()
+        pl.when(with_down)(w_right[1][0].start)
+        w_pair[1].wait_recv()
+        w_left[1][1].start()
+        w_right[1][1].start()
+        pl.when(with_down)(w_left[1][0].start)
+        w_core[0][1].start()
+
+    pl.when(c == 1)(pair_arrived)
     pass_on(0)
-    loads[3].wait()
+    pl.when(c == 0)(pair_arrived)
+    pump(1)
+
+    def ws_spread():
+        ws_far.wait_recv()
+        ws_cross.wait_recv()
+        for copy in ws_x:
+            copy.start()
+        ws_core[0].start()
+
+    def ws_pass_on():
+        for o in (1, 3, 2):
+            ws_x[o - 1].wait_recv()
+            ws_core[o].start()
+
+    def ws_ready():
+        for o in (0, 1, 3, 2):
+            ws_core[o].wait_recv()
+
+    def gain_ready():
+        gain_copy.wait_recv()
+        gain_far[...] = gain_land[...].astype(f32)
+
+    pl.when(s == 0)(ws_spread)
+    loads[4].wait()
     group_ready(0)
     delta = add_delta(0, jnp.zeros((ROWS, RANK), f32))
     pass_on(1)
-    gain_copy.wait_recv()
-    gain_far[...] = gain_land[...].astype(f32)
     group_ready(1)
     delta = add_delta(1, delta)
+    end_group(0)
     group_ready(3)
-    delta = add_delta(3, delta)
-    end_group(0)
-    lax.fori_loop(0, 2, write_normed, 0)
-    end_group(1)
-    ws_far.wait_recv()
-    ws_cross.wait_recv()
-    for copy in ws_x:
-        copy.start()
-    ws_core[0].start()
-    group_ready(2)
-    delta = add_delta(2, delta)
-    delta_own[...] = jnp.zeros((ROWS, 128), bf16)
-    delta_own[:, :RANK] = delta.astype(bf16)
-    delta_copy.start()
+    delta_sum[...] = add_delta(3, delta)
+
+    def finish_delta():
+        end_group(1)
+        group_ready(2)
+        delta_own[...] = jnp.zeros((ROWS, 128), bf16)
+        delta_own[:, :RANK] = add_delta(2, delta_sum[...]).astype(bf16)
+        delta_copy.start()
+
+    pl.when(s != 0)(finish_delta)
+    pl.when(s == 8)(base_half(1).start)
     pump(2)
 
     def fill_b(start, count):
@@ -314,8 +342,20 @@
         b_sum = lax.fori_loop(0, 4, write_b, jnp.zeros((count, 128), f32))
         b_mean[rows, :] = row_sum(b_sum) * (1.0 / D)
 
-    loads[4].wait()
-    fill_b(0, 2 * CHUNK)
+    pl.when(s != 0)(base_load.wait)
+
+    @pl.when(with_down)
+    def _():
+        fill_b(0, 2 * CHUNK)
+
+    @pl.when(s == 0)
+    def _():
+        ws_pass_on()
+        ws_ready()
+        gain_ready()
+        delta_copy.wait_recv()
+        saved_load.wait()
+
 
     def grad_chunk(k):
         rows = chunk_rows(k)
@@ -331,44 +371,53 @@
 
         lax.fori_loop(0, WIDES, one, 0)
 
+    def fill_far(k):
+        rows = chunk_rows(k)
+
+        def write_far(g, acc):
+            for i in range(4):
+                e = g * 4 + i
+                cols = columns(feature(e))
+                back = jnp.dot(delta_far[rows, :RANK], WS[e], preferred_element_type=f32)
+                value = (ba[rows, cols].astype(f32) + back) * gain_far[:, cols]
+                b[rows, cols] = value
+                acc = acc + fold(value)
+            return acc
+
+        b_sum = lax.fori_loop(0, 4, write_far, jnp.zeros((CHUNK, 128), f32))
+        b_mean[rows, :] = row_sum(b_sum) * (1.0 / D)
+
     def step(k):
-        @pl.when(s != 0)
+        @pl.when(s == 0)
+        def _():
+            for copy in (base_half(0), base_half(1)) if k == 1 else (base_copy(k),):
+                copy.wait_recv()
+            fill_far(k)
+
+        @pl.when(jnp.logical_and(s != 0, s != 8))
         def _():
             stash_copy(k).wait_recv()
+
+        @pl.when(s != 8)
+        def _():
             grad_chunk(k)
-
-        @pl.when(s == 8)
-        def _():
-            if k == CHUNKS - 1:
-                direct_copy(k).start()
-            else:
-                for i in range(PARTS):
-                    relay_part(k, i).start()
-
-        @pl.when(jnp.logical_and(s != 0, s != 8))
-        def _():
             z_copy(k).start()
 
-        if k > 0:
-            relay(k - 1)
-
-    def relay(k):
-        @pl.when(s == 0)
-        def _():
-            for i in range(PARTS):
-                relay_part(k, i).wait_recv()
-                z_part(k, i).start()
-
     step(0)
-    fill_b(2 * CHUNK, ROWS - 2 * CHUNK)
-    lax.fori_loop(2, CHUNKS, write_normed, 0)
+    pl.when(s != 0)(ws_spread)
+
+    @pl.when(with_down)
+    def _():
+        fill_b(2 * CHUNK, ROWS - 2 * CHUNK)
+
     step(1)
-
-    for o in (1, 3, 2):
-        ws_x[o - 1].wait_recv()
-        ws_core[o].start()
-    for o in (0, 1, 3, 2):
-        ws_core[o].wait_recv()
+    pump(3)
+    pl.when(s == 0)(finish_delta)
+    pl.when(s != 0)(gain_ready)
+    lax.fori_loop(0, CHUNKS, write_normed, 0)
+    pl.when(s != 0)(ws_pass_on)
+    step(2)
+    pl.when(s != 0)(ws_ready)
 
     def add_low(g, acc):
         for i in range(4):
@@ -380,12 +429,11 @@
     low_own[...] = jnp.zeros((ROWS, 128), bf16)
     low_own[:, :RANK] = low.astype(bf16)
     low_copy.start()
-    pump(3)
-    pump_rest()
-    step(2)
     pump(4)
-
-    delta_copy.wait_recv()
+    step(3)
+    pump(5)
+    pl.when(s != 0)(delta_copy.wait_recv)
+
     low_copy.wait_recv()
     delta_t = delta_far[...].astype(f32).T[:RANK].astype(bf16)
     low_t = low_far[...].astype(f32).T[:RANK].astype(bf16)
@@ -402,9 +450,9 @@
 
     lax.fori_loop(0, 8, write_parts, 0)
     part_copy.start()
-    step(3)
-    pump(5)
-
+
+    step(4)
+    pump(6)
     part_copy.wait_recv()
 
     def add_parts(j, carry):
@@ -416,10 +464,9 @@
     for copy in sum_copy:
         copy.start()
 
-    step(4)
-    pump(6)
     step(5)
     pump(7)
+    step(6)
 
     for copy in sum_copy:
         copy.wait_recv()
@@ -430,22 +477,25 @@
             total = total + sum_recv[i, y, kind].astype(f32)
         return total
 
-    for kind in range(2):
-        pair_send[kind] = total_of(1 - yl, kind).astype(bf16)
-        kept[kind] = total_of(yl, kind)
-    pair_copy.start()
-
-    step(6)
+    total_send[0] = total_of(yl, 0).astype(bf16)
+    total_send[1] = total_of(1 - yl, 0).astype(bf16)
+    total_send[2] = total_of(1 - yl, 1).astype(bf16)
+    kept[...] = total_of(yl, 1)
+    for copy in total_copy:
+        copy.start()
+
     step(7)
 
-    pair_copy.wait_recv()
-    final_send[...] = (kept[0] + pair_recv[0].astype(f32)).astype(bf16)
-    final_copy.start()
-    loads[7].wait()
-    step2[...], new2[...] = lion(m2[...].astype(f32), kept[1] + pair_recv[1].astype(f32))
-    final_copy.wait_recv()
+    for copy in total_copy:
+        copy.wait_recv()
+    loads[5].wait()
     loads[6].wait()
-    step1[...], new1[...] = lion(m1[...].astype(f32), final_recv[...].astype(f32))
+    grad_first = total_recv[0].astype(f32) + total_recv[1].astype(f32)
+    results[0], results[2] = lion(m1[...].astype(f32), grad_first)
+    results[1], results[3] = lion(m2[...].astype(f32), kept[...] + total_recv[2].astype(f32))
+    stores = [pltpu.make_async_copy(results.at[i], out, local_sem.at[9 + i]) for i, out in enumerate((step1, step2, new1, new2))]
+    for store in stores:
+        store.start()
 
     @pl.when(s == 15)
     def _():
@@ -454,28 +504,35 @@
         zeros.start()
         zeros.wait()
 
-    sent = [w_pair, *w_right, *w_left, *w_on_right, *w_on_left, ws_far, ws_cross, *ws_x, *ws_core]
+    for store in stores:
+        store.wait()
+
+    down_sent = [w_right[0][0], w_right[1][0], w_left[0][0], w_left[1][0], *w_on_right]
+    sent = [*w_pair, w_right[0][1], w_right[1][1], w_left[0][1], w_left[1][1], *w_on_left, ws_far, ws_cross, *ws_x, *ws_core]
     sent += [copy for pair_of in w_core for copy in pair_of]
-    sent += [gain_copy, delta_copy, low_copy, part_copy, *sum_copy, pair_copy, final_copy]
+    sent += [gain_copy, delta_copy, low_copy, part_copy, *sum_copy, *total_copy]
     for copy in sent:
         copy.wait_send()
+
+    @pl.when(with_down)
+    def _():
+        for copy in down_sent:
+            copy.wait_send()
+
     for k in range(CHUNKS):
+        @pl.when(s != 0 if k != 1 else with_down)
+        def _():
+            stash_copy(k).wait_send()
+
+        if k == 1:
+            @pl.when(s == 8)
+            def _():
+                base_half(0).wait_send()
+                base_half(1).wait_send()
+
         @pl.when(s != 8)
         def _():
-            stash_copy(k).wait_send()
-            if k < CHUNKS - 1:
-                z_copy(k).wait_send()
-
-        @pl.when(s == 8)
-        def _():
-            if k < CHUNKS - 1:
-                for i in range(PARTS):
-                    relay_part(k, i).wait_send()
-
-        if k == CHUNKS - 1:
-            @pl.when(s != 0)
-            def _():
-                z_copy(k).wait_send()
+            z_copy(k).wait_send()
 
         @pl.when(s != 15)
         def _():
@@ -500,7 +557,6 @@
 
 def shards(stash, grad_in, base_back, gain, w_down, w_up, mom_down, mom_up):
     hbm = pl.BlockSpec(memory_space=pltpu.HBM)
-    vmem = pl.BlockSpec(memory_space=pltpu.VMEM)
     share = (RANK, SHARE)
     maps = jax.ShapeDtypeStruct(share, bf16)
     shapes = (jax.ShapeDtypeStruct((ROWS, D), bf16), maps, maps, maps, maps)
@@ -508,8 +564,9 @@
         main_kernel,
         out_shape=shapes,
         in_specs=[hbm] * 8,
-        out_specs=(hbm, vmem, vmem, vmem, vmem),
+        out_specs=(hbm,) * 5,
         scratch_shapes=[
+            pltpu.VMEM((4,) + share, bf16),
             pltpu.VMEM(share, bf16),
             pltpu.VMEM(share, bf16),
             pltpu.VMEM((1, D), bf16),
@@ -523,6 +580,7 @@
             pltpu.VMEM((16,) + share, bf16),
             pltpu.VMEM((1, D), f32),
             pltpu.VMEM((1, D), f32),
+            pltpu.VMEM((ROWS, RANK), f32),
             pltpu.VMEM((ROWS, 128), bf16),
             pltpu.VMEM((ROWS, 128), bf16),
             pltpu.VMEM((ROWS, 128), bf16),
@@ -535,12 +593,10 @@
             pltpu.VMEM((8, 2) + share, bf16),
             pltpu.VMEM((4, 2, 2) + share, bf16),
             pltpu.VMEM((3, 2, 2) + share, bf16),
-            pltpu.VMEM((2,) + share, bf16),
-            pltpu.VMEM((2,) + share, bf16),
-            pltpu.VMEM((2,) + share, f32),
-            pltpu.VMEM(share, bf16),
-            pltpu.VMEM(share, bf16),
-            pltpu.SemaphoreType.DMA((9,)),
+            pltpu.VMEM((3,) + share, bf16),
+            pltpu.VMEM((3,) + share, bf16),
+            pltpu.VMEM(share, f32),
+            pltpu.SemaphoreType.DMA((13,)),
             pltpu.SemaphoreType.DMA((SEMS,)),
             pltpu.SemaphoreType.DMA((SEMS,)),
         ],

time: 109 us -> 106 us (0.972)
  Pallas kernels: 108 us -> 105 us
    pallas_call x1, Pallas kernels: 105 us -> 102 us  [shards(): pl.pallas_call(main_kernel, out_shape=shapes, in_specs=[hbm] * 8, out_spe...]
where the time goes in v3:
time: 106 us
  Pallas kernels  105 us (99%)
    pallas_call x1, Pallas kernels, shards(): pl.pallas_call(main_kernel, out_shape=shapes, in_specs=[hbm] * 8, out_spe...  102 us
    pallas_call x1, Pallas kernels, shards(): pl.pallas_call(finish_kernel, out_shape=shapes, in_specs=[hbm] * 5, out_s...  3.29 us

profile of v3, /device:TPU:1, one launch (start us, length us, event | category | flops | bytes accessed | tf_op | source)
XLA Modules:
  0.0 106.1 jit_solution(1788126013723176019)
XLA Ops:
  0.6 102.2 %block.1 = (bf16[128,12288]{1,0:T(8,128)(2,1)}, bf16[64,768]{1,0:T(8,128)(2,1)}, bf16[64,768]{1,0:T(8,128)(2,1)}, bf16[64,768]{1,0:T(8,128)(2,1)}, bf16[64,768]{1,0:T(8,128)(2,1)}) custom-call(bf16[128,12288]{1,0:T(8,128)(2,1)} %bitcast.8, bf16[128,12288]{1,0:T(8,128)(2,1)} %bitcast.9, bf16[128,12288]{1,0:T(8,128)(2,1)} %bitcast.10, bf16[1,12288]{1,0:T(2,128)(2,1)} %gain.1, ...), custom_call_target="tpu_custom_call" | custom-call | flops 1006632960 | bytes 25165824 | tf_op jit(solution)/shard_map/block/pallas_call | solution.py:563
  102.8 3.3 %finish.1 = (bf16[128,12288]{1,0:T(8,128)(2,1)}, bf16[64,768]{1,0:T(8,128)(2,1)}, bf16[64,768]{1,0:T(8,128)(2,1)}, bf16[64,768]{1,0:T(8,128)(2,1)}, bf16[64,768]{1,0:T(8,128)(2,1)}) custom-call(bf16[128,12288]{1,0:T(8,128)(2,1)} %get-tuple-element.15.rows, bf16[64,768]{1,0:T(8,128)(2,1)} %get-tuple-element.16.a, bf16[64,768]{1,0:T(8,128)(2,1)} %get-tuple-element.17.b, ...), custom_call_target="tpu_custom_call" | custom-call | tf_op jit(solution)/shard_map/finish/pallas_call | solution.py:609

commit v4 on v3

--- a/solution.py
+++ b/solution.py
@@ -55,6 +55,23 @@
     direction = (blend / (jnp.abs(blend) + lion_delta)).astype(bf16)
     renewed = (beta_two * moment + (1.0 - beta_two) * gradient).astype(bf16)
     return direction, renewed
+
+
+class Either:
+    def __init__(self, chosen, one, other):
+        self.pairs = ((chosen, one), (jnp.logical_not(chosen), other))
+
+    def start(self):
+        for flag, copy in self.pairs:
+            pl.when(flag)(copy.start)
+
+    def wait_recv(self):
+        for flag, copy in self.pairs:
+            pl.when(flag)(copy.wait_recv)
+
+    def wait_send(self):
+        for flag, copy in self.pairs:
+            pl.when(flag)(copy.wait_send)
 
 
 def main_kernel(
@@ -145,8 +162,9 @@
         return WS.at[pl.ds(xs * 4 + c * 2, 2)]
 
     def core_copy(o, kind):
-        slot = W.at[slot_of(o, kind)]
-        return remote(slot, slot, CORE + 2 * o + kind, (s, d_core))
+        slot, up = W.at[slot_of(o, kind)], W.at[slot_of(o, kind), 1]
+        both = remote(slot, slot, CORE + 2 * o + kind, (s, d_core))
+        return Either(with_down, both, remote(up, up, CORE + 2 * o + kind, (s, d_core)))
 
     x_from = [(x + 4 - o) % 4 for o in range(4)]
     w_core = [[core_copy(o, kind) for kind in range(2)] for o in range(4)]
@@ -177,18 +195,18 @@
 
     loads[0].wait()
     loads[1].wait()
-    pl.when(s == 8)(ws_far.start)
-    w_pair[0].start()
+    loads[2].wait()
+    gain_copy.start()
+    ws_cross.start()
+    pl.when(with_down)(w_pair[0].start)
     w_pair[1].start()
+    pl.when(jnp.logical_not(with_down))(w_pair[0].start)
     pl.when(with_down)(w_right[0][0].start)
     w_left[0][1].start()
     w_right[0][1].start()
     pl.when(with_down)(w_left[0][0].start)
-    pl.when(s != 8)(ws_far.start)
+    ws_far.start()
     w_core[0][0].start()
-    loads[2].wait()
-    gain_copy.start()
-    ws_cross.start()
 
     def pump(k):
         @pl.when(jnp.logical_and(s != 0, s != 8))
@@ -271,7 +289,7 @@
         return lax.fori_loop(0, WIDES, one, carry)
 
     def pair_arrived():
-        w_pair[0].wait_recv()
+        pl.when(with_down)(w_pair[0].wait_recv)
         pl.when(with_down)(w_right[1][0].start)
         w_pair[1].wait_recv()
         w_left[1][1].start()
@@ -511,6 +529,7 @@
     sent = [*w_pair, w_right[0][1], w_right[1][1], w_left[0][1], w_left[1][1], *w_on_left, ws_far, ws_cross, *ws_x, *ws_core]
     sent += [copy for pair_of in w_core for copy in pair_of]
     sent += [gain_copy, delta_copy, low_copy, part_copy, *sum_copy, *total_copy]
+    pl.when(jnp.logical_not(with_down))(w_pair[0].wait_recv)
     for copy in sent:
         copy.wait_send()
 

time: 106 us -> 103 us (0.972)
  Pallas kernels: 105 us -> 102 us
    pallas_call x1, Pallas kernels: 102 us -> 99 us  [shards(): pl.pallas_call(main_kernel, out_shape=shapes, in_specs=[hbm] * 8, out_spe...]
where the time goes in v4:
time: 103 us
  Pallas kernels  102 us (99%)
    pallas_call x1, Pallas kernels, shards(): pl.pallas_call(main_kernel, out_shape=shapes, in_specs=[hbm] * 8, out_spe...  99 us
    pallas_call x1, Pallas kernels, shards(): pl.pallas_call(finish_kernel, out_shape=shapes, in_specs=[hbm] * 5, out_s...  3.29 us

profile of v4, /device:TPU:1, one launch (start us, length us, event | category | flops | bytes accessed | tf_op | source)
XLA Modules:
  0.0 102.9 jit_solution(2626712777970234419)
XLA Ops:
  0.6 99.0 %block.1 = (bf16[128,12288]{1,0:T(8,128)(2,1)}, bf16[64,768]{1,0:T(8,128)(2,1)}, bf16[64,768]{1,0:T(8,128)(2,1)}, bf16[64,768]{1,0:T(8,128)(2,1)}, bf16[64,768]{1,0:T(8,128)(2,1)}) custom-call(bf16[128,12288]{1,0:T(8,128)(2,1)} %bitcast.8, bf16[128,12288]{1,0:T(8,128)(2,1)} %bitcast.9, bf16[128,12288]{1,0:T(8,128)(2,1)} %bitcast.10, bf16[1,12288]{1,0:T(2,128)(2,1)} %gain.1, ...), custom_call_target="tpu_custom_call" | custom-call | flops 1006632960 | bytes 25165824 | tf_op jit(solution)/shard_map/block/pallas_call | solution.py:582
  99.6 3.3 %finish.1 = (bf16[128,12288]{1,0:T(8,128)(2,1)}, bf16[64,768]{1,0:T(8,128)(2,1)}, bf16[64,768]{1,0:T(8,128)(2,1)}, bf16[64,768]{1,0:T(8,128)(2,1)}, bf16[64,768]{1,0:T(8,128)(2,1)}) custom-call(bf16[128,12288]{1,0:T(8,128)(2,1)} %get-tuple-element.15.rows, bf16[64,768]{1,0:T(8,128)(2,1)} %get-tuple-element.16.a, bf16[64,768]{1,0:T(8,128)(2,1)} %get-tuple-element.17.b, ...), custom_call_target="tpu_custom_call" | custom-call | tf_op jit(solution)/shard_map/finish/pallas_call | solution.py:628
